TPU v7x, 32 devices: a whole 2x2x4 slice. The times are simulated.
32 devices in a mesh: mic: 4 (over z), tm: 8 (over y, x, core).
Axes of the slice: x: 2, y: 2, z: 4, core: 2. Of those that a mesh axis runs over, the one named last changes fastest.
Arguments:
- signal: float32 [4, 8192, 512], P('mic', 'tm'), may hold values from -6 to 6
- conv_weight: float32 [2, 3, 2, 512, 512], replicated, may hold values from -0.1875 to 0.1875
- conv_bias: float32 [2, 3, 512], replicated, may hold values from -3 to 3
- transform_in: float32 [2, 512, 512], replicated, may hold values from -0.25 to 0.25
- transform_mid: float32 [2, 512, 512], replicated, may hold values from -0.25 to 0.25
- transform_out: float32 [2, 1024, 512], replicated, may hold values from -0.1875 to 0.1875
- transform_offsets_bias: float32 [2, 3, 512], replicated, may hold values from -3 to 3
Outputs:
- separated: float32 [4, 8192, 512], P('mic', 'tm')
All inputs are finite; a program needn't handle non-finite values.
Results may differ from a plain program's by a relative error of at most 0.0001.
Values sent between devices are 32-bit elements; how exact they have to be, the bound alone decides.
A program may use at most 128 MiB of HBM per device.

v0:
```python
import jax
import jax.numpy as jnp
from jax import lax
from jax.sharding import PartitionSpec as P

SEPARATOR_BLOCKS = 2


def from_behind(x, axis, by):
    length = lax.axis_size(axis)
    pairs = [(i, i + by) for i in range(length) if 0 <= i + by < length]
    return lax.ppermute(x, axis, pairs)


def matmul(left, right):
    return jnp.dot(left, right, precision=lax.Precision.HIGHEST, preferred_element_type=jnp.float32)


def convolve(hidden_activations, weights, bias, delayed):
    return hidden_activations + jnp.tanh(
        matmul(hidden_activations, weights[0]) + matmul(delayed, weights[1]) + bias
    )


def body(
    signal,
    conv_weight,
    conv_bias,
    transform_in,
    transform_mid,
    transform_out,
    transform_offsets_bias,
):
    hidden_activations = signal[0]
    frames = hidden_activations.shape[0]
    half = frames // 2
    channels = hidden_activations.shape[1]
    micro_count = jnp.float32(lax.axis_size("mic") * signal.shape[0])
    for section_index in range(SEPARATOR_BLOCKS):
        earlier = from_behind(hidden_activations[frames - half :], "tm", 1)
        delayed = jnp.concatenate([earlier, hidden_activations[: frames - half]], axis=0)
        hidden_activations = convolve(
            hidden_activations, conv_weight[section_index, 0], conv_bias[section_index, 0], delayed
        )
        delayed = from_behind(hidden_activations, "tm", 1)
        hidden_activations = convolve(
            hidden_activations, conv_weight[section_index, 1], conv_bias[section_index, 1], delayed
        )
        delayed = from_behind(hidden_activations, "tm", 2)
        hidden_activations = convolve(
            hidden_activations, conv_weight[section_index, 2], conv_bias[section_index, 2], delayed
        )
        mapped = jnp.tanh(
            matmul(hidden_activations, transform_in[section_index])
            + transform_offsets_bias[section_index, 0]
        )
        summed = lax.psum(mapped, "mic")
        pooled = jnp.tanh(
            matmul(summed / micro_count, transform_mid[section_index])
            + transform_offsets_bias[section_index, 1]
        )
        mixing = (
            matmul(mapped, transform_out[section_index, :channels])
            + matmul(pooled, transform_out[section_index, channels:])
            + transform_offsets_bias[section_index, 2]
        )
        hidden_activations = hidden_activations + jnp.tanh(mixing)
    return hidden_activations[None]


def solution(mesh):
    placed = (P("mic", "tm", None), P(), P(), P(), P(), P(), P())
    return jax.shard_map(
        body, mesh=mesh, in_specs=placed, out_specs=P("mic", "tm", None), check_vma=False
    )
```

profile of v0, /device:TPU:0, one launch (start us, length us, event | category | flops | bytes accessed | tf_op | source)
XLA Modules:
  0.0 441.6 jit_solution(17344065074883003258)
XLA Ops:
  15.6 4.9 %bitcast_add_fusion = f32[1024,512]{1,0:T(8,128)S(1)} fusion(f32[1,1024,512]{2,1,0:T(8,128)S(1)} %copy-done.2, f32[1024,512]{1,0:T(8,128)S(1)} %fusion.8, f32[512,512]{1,0:T(8,128)S(1)} %get-tuple-element.8, f32[512,512]{1,0:T(8,128)S(1)} %collective-permute-done, f32[512]{0:T(512)S(1)} %bitcast.106, f32[2,3,2,512,512]{4,3,2,1,0:T(8,128)} %param.8), kind=kOutput, calls=%fused_computation.8 | convolution fusion | flops 3223322624 | bytes 9439232 | tf_op jit(solution)/shard_map/dot_general | solution.py:16
  20.5 11.8 %collective-permute-start.1 = (f32[1024,512]{1,0:T(8,128)S(1)}, f32[1024,512]{1,0:T(8,128)S(1)}, u32[]{:S(2)}, u32[]{:S(2)}) collective-permute-start(f32[1024,512]{1,0:T(8,128)S(1)} %bitcast_add_fusion), channel_id=1, source_target_pairs={{0,1},{1,2},{2,3},{3,4},{4,5},{5,6},{6,7},{8,9},{9,10},{10,11},{11... | collective-permute-start | bytes 6291464 | tf_op jit(solution)/shard_map/ppermute | solution.py:12
  32.3 4.7 %fusion.45 = f32[1024,512]{1,0:T(8,128)S(1)} fusion(f32[1024,512]{1,0:T(8,128)S(1)} %bitcast_add_fusion, f32[2,3,2,512,512]{4,3,2,1,0:T(8,128)} %param.8), kind=kOutput, calls=%fused_computation.51 | convolution fusion | flops 3221225472 | bytes 5242880 | tf_op jit(solution)/shard_map/dot_general | solution.py:16
  37.0 4.9 %tanh_add_fusion.5 = f32[1024,512]{1,0:T(8,128)S(1)} fusion(f32[1024,512]{1,0:T(8,128)S(1)} %bitcast_add_fusion, f32[1024,512]{1,0:T(8,128)S(1)} %fusion.45, f32[1024,512]{1,0:T(8,128)S(1)} %collective-permute-done.1, f32[512]{0:T(512)S(1)} %bitcast.104, f32[2,3,2,512,512]{4,3,2,1,0:T(8,128)} %param.8), kind=kOutput, calls=%fused_computation.29 | convolution fusion | flops 3222798336 | bytes 9439232 | tf_op jit(solution)/shard_map/dot_general | solution.py:16
  42.0 25.1 %collective-permute-start.2 = (f32[1024,512]{1,0:T(8,128)S(1)}, f32[1024,512]{1,0:T(8,128)S(1)}, u32[]{:S(2)}, u32[]{:S(2)}) collective-permute-start(f32[1024,512]{1,0:T(8,128)S(1)} %tanh_add_fusion.5), channel_id=1, source_target_pairs={{0,2},{1,3},{2,4},{3,5},{4,6},{5,7},{8,10},{9,11},{10,12},{11,13},... | collective-permute-start | bytes 6291464 | tf_op jit(solution)/shard_map/ppermute | solution.py:12
  67.1 4.7 %fusion.42 = f32[1024,512]{1,0:T(8,128)S(1)} fusion(f32[1024,512]{1,0:T(8,128)S(1)} %tanh_add_fusion.5, f32[2,3,2,512,512]{4,3,2,1,0:T(8,128)} %param.8), kind=kOutput, calls=%fused_computation.48 | convolution fusion | flops 3221225472 | bytes 5242880 | tf_op jit(solution)/shard_map/dot_general | solution.py:16
  71.8 39.9 %collective-permute-done.2 = f32[1024,512]{1,0:T(8,128)S(1)} collective-permute-done((f32[1024,512]{1,0:T(8,128)S(1)}, f32[1024,512]{1,0:T(8,128)S(1)}, u32[]{:S(2)}, u32[]{:S(2)}) %collective-permute-start.2) | collective-permute-done | bytes 2097184 | tf_op jit(solution)/shard_map/ppermute | solution.py:12
  111.7 5.1 %tanh_add_fusion.4 = f32[1024,512]{1,0:T(8,128)S(1)} fusion(f32[1024,512]{1,0:T(8,128)S(1)} %tanh_add_fusion.5, f32[1024,512]{1,0:T(8,128)S(1)} %fusion.42, f32[1024,512]{1,0:T(8,128)S(1)} %collective-permute-done.2, f32[512]{0:T(512)S(1)} %bitcast.101, f32[2,3,2,512,512]{4,3,2,1,0:T(8,128)} %param.8), kind=kOutput, calls=%fused_computation.28 | convolution fusion | flops 3222798336 | bytes 9439232 | tf_op jit(solution)/shard_map/dot_general | solution.py:16
  116.8 4.8 %add_tanh_fusion.1 = f32[1024,512]{1,0:T(8,128)} fusion(f32[1024,512]{1,0:T(8,128)S(1)} %tanh_add_fusion.4, f32[512]{0:T(512)S(1)} %bitcast.105, f32[2,512,512]{2,1,0:T(8,128)S(1)} %copy-done.5), kind=kOutput, calls=%fused_computation.27 | convolution fusion | flops 3221749760 | bytes 5244928 | tf_op jit(solution)/shard_map/dot_general | solution.py:16
  122.1 87.5 %all-reduce.3.cloned.1.call-done = f32[1024,512]{1,0:T(8,128)} async-done(((f32[1024,512]{1,0:T(8,128)}), f32[1024,512]{1,0:T(8,128)}) %all-reduce.3.cloned.1.call-update) | async-done | bytes 2097168 | tf_op jit(solution)/shard_map/psum | solution.py:57
  209.6 5.5 %fusion.18 = f32[1024,512]{1,0:T(8,128)S(1)} fusion(f32[1024,512]{1,0:T(8,128)} %all-reduce.3.cloned.1.call-done, f32[2,512,512]{2,1,0:T(8,128)} %param.11), kind=kOutput, calls=%fused_computation.25 | convolution fusion | flops 3221749760 | bytes 5242880 | tf_op jit(solution)/shard_map/dot_general | solution.py:16
  224.6 4.7 %fusion.35 = f32[1024,512]{1,0:T(8,128)S(1)} fusion(f32[1024,512]{1,0:T(8,128)S(1)} %tanh_add_fusion.3, f32[2,3,2,512,512]{4,3,2,1,0:T(8,128)} %param.8), kind=kOutput, calls=%fused_computation.41 | convolution fusion | flops 3221225472 | bytes 5242880 | tf_op jit(solution)/shard_map/dot_general | solution.py:16
  229.2 5.0 %tanh_add_fusion.2 = f32[1024,512]{1,0:T(8,128)S(1)} fusion(f32[1024,512]{1,0:T(8,128)S(1)} %tanh_add_fusion.3, f32[1024,512]{1,0:T(8,128)S(1)} %fusion.35, f32[512,512]{1,0:T(8,128)S(1)} %get-tuple-element.6, f32[512,512]{1,0:T(8,128)S(1)} %collective-permute-done.3, f32[512]{0:T(512)S(1)} %bitcast.99, f32[2,3,2,512,512]{4,3,2,1,0:T(8,128)} %param.8), kind=kOutput, calls=%fused_computation.20 | convolution fusion | flops 3223322624 | bytes 9439232 | tf_op jit(solution)/shard_map/dot_general | solution.py:16
  234.2 10.6 %collective-permute-start.4 = (f32[1024,512]{1,0:T(8,128)S(1)}, f32[1024,512]{1,0:T(8,128)S(1)}, u32[]{:S(2)}, u32[]{:S(2)}) collective-permute-start(f32[1024,512]{1,0:T(8,128)S(1)} %tanh_add_fusion.2), channel_id=1, source_target_pairs={{0,1},{1,2},{2,3},{3,4},{4,5},{5,6},{6,7},{8,9},{9,10},{10,11},{11... | collective-permute-start | bytes 6291464 | tf_op jit(solution)/shard_map/ppermute | solution.py:12
  244.8 4.7 %fusion.32 = f32[1024,512]{1,0:T(8,128)S(1)} fusion(f32[1024,512]{1,0:T(8,128)S(1)} %tanh_add_fusion.2, f32[2,3,2,512,512]{4,3,2,1,0:T(8,128)} %param.8), kind=kOutput, calls=%fused_computation.38 | convolution fusion | flops 3221225472 | bytes 5242880 | tf_op jit(solution)/shard_map/dot_general | solution.py:16
  249.5 4.9 %tanh_add_fusion.1 = f32[1024,512]{1,0:T(8,128)S(1)} fusion(f32[1024,512]{1,0:T(8,128)S(1)} %tanh_add_fusion.2, f32[1024,512]{1,0:T(8,128)S(1)} %fusion.32, f32[1024,512]{1,0:T(8,128)S(1)} %collective-permute-done.4, f32[512]{0:T(512)S(1)} %bitcast.97, f32[2,3,2,512,512]{4,3,2,1,0:T(8,128)} %param.8), kind=kOutput, calls=%fused_computation.19 | convolution fusion | flops 3222798336 | bytes 9439232 | tf_op jit(solution)/shard_map/dot_general | solution.py:16
  254.4 25.2 %collective-permute-start.5 = (f32[1024,512]{1,0:T(8,128)S(1)}, f32[1024,512]{1,0:T(8,128)S(1)}, u32[]{:S(2)}, u32[]{:S(2)}) collective-permute-start(f32[1024,512]{1,0:T(8,128)S(1)} %tanh_add_fusion.1), channel_id=1, source_target_pairs={{0,2},{1,3},{2,4},{3,5},{4,6},{5,7},{8,10},{9,11},{10,12},{11,13},... | collective-permute-start | bytes 6291464 | tf_op jit(solution)/shard_map/ppermute | solution.py:12
  279.7 4.7 %fusion.29 = f32[1024,512]{1,0:T(8,128)S(1)} fusion(f32[1024,512]{1,0:T(8,128)S(1)} %tanh_add_fusion.1, f32[2,3,2,512,512]{4,3,2,1,0:T(8,128)} %param.8), kind=kOutput, calls=%fused_computation.35 | convolution fusion | flops 3221225472 | bytes 5242880 | tf_op jit(solution)/shard_map/dot_general | solution.py:16
  284.4 40.0 %collective-permute-done.5 = f32[1024,512]{1,0:T(8,128)S(1)} collective-permute-done((f32[1024,512]{1,0:T(8,128)S(1)}, f32[1024,512]{1,0:T(8,128)S(1)}, u32[]{:S(2)}, u32[]{:S(2)}) %collective-permute-start.5) | collective-permute-done | bytes 2097184 | tf_op jit(solution)/shard_map/ppermute | solution.py:12
  324.4 5.1 %tanh_add_fusion = f32[1024,512]{1,0:T(8,128)S(1)} fusion(f32[1024,512]{1,0:T(8,128)S(1)} %tanh_add_fusion.1, f32[1024,512]{1,0:T(8,128)S(1)} %fusion.29, f32[1024,512]{1,0:T(8,128)S(1)} %collective-permute-done.5, f32[512]{0:T(512)S(1)} %bitcast.95, f32[2,3,2,512,512]{4,3,2,1,0:T(8,128)} %param.8), kind=kOutput, calls=%fused_computation.18 | convolution fusion | flops 3222798336 | bytes 9439232 | tf_op jit(solution)/shard_map/dot_general | solution.py:16
  329.5 4.8 %add_tanh_fusion = f32[1024,512]{1,0:T(8,128)} fusion(f32[1024,512]{1,0:T(8,128)S(1)} %tanh_add_fusion, f32[512]{0:T(512)S(1)} %bitcast.100, f32[2,512,512]{2,1,0:T(8,128)S(1)} %copy-done.6), kind=kOutput, calls=%fused_computation.17 | convolution fusion | flops 3221749760 | bytes 5244928 | tf_op jit(solution)/shard_map/dot_general | solution.py:16
  334.3 85.7 %all-reduce.5.cloned.1.call-done = f32[1024,512]{1,0:T(8,128)} async-done(((f32[1024,512]{1,0:T(8,128)}), f32[1024,512]{1,0:T(8,128)}) %all-reduce.5.cloned.1.call-update) | async-done | bytes 2097168 | tf_op jit(solution)/shard_map/psum | solution.py:57
  420.0 5.7 %fusion.13 = f32[1024,512]{1,0:T(8,128)S(1)} fusion(f32[1024,512]{1,0:T(8,128)} %all-reduce.5.cloned.1.call-done, f32[2,512,512]{2,1,0:T(8,128)} %param.11), kind=kOutput, calls=%fused_computation.15 | convolution fusion | flops 3221749760 | bytes 5242880 | tf_op jit(solution)/shard_map/dot_general | solution.py:16
  429.3 5.0 %add_bitcast_fusion = f32[1,1024,512]{2,1,0:T(8,128)} fusion(f32[1024,512]{1,0:T(8,128)S(1)} %tanh_add_fusion, f32[1024,512]{1,0:T(8,128)S(1)} %fusion.10, f32[1024,512]{1,0:T(8,128)S(1)} %copy-done.1, f32[512]{0:T(512)S(1)} %bitcast.96, f32[2,1024,512]{2,1,0:T(8,128)S(1)} %copy-done.4), kind=kOutput, calls=%fused_computation.11 | convolution fusion | flops 3222798336 | bytes 9439232 | tf_op jit(solution)/shard_map/dot_general | solution.py:16
  (36 shorter events, 22.5 us)
Async XLA Ops:
  6.5 4.3 copy-start.2
  6.5 4.3 copy-start.7
  6.5 203.0 %all-reduce.3.cloned.1.call-start = ((), (), s32[]{:S(2)}) async-start(), calls=%async_computation | async-start | bytes 4194304 | tf_op jit(solution)/shard_map/psum | solution.py:57
  8.4 7.1 %collective-permute-start = (f32[512,512]{1,0:T(8,128)S(1)}, f32[512,512]{1,0:T(8,128)S(1)}, u32[]{:S(2)}, u32[]{:S(2)}) collective-permute-start(f32[512,512]{1,0:T(8,128)S(1)} %get-tuple-element.7), channel_id=1, source_target_pairs={{0,1},{1,2},{2,3},{3,4},{4,5},{5,6},{6,7},{8,9},{9,10},{10,11},{11... | collective-permute-start | bytes 3145736 | tf_op jit(solution)/shard_map/ppermute | solution.py:12
  20.5 16.5 %collective-permute-start.1 = (f32[1024,512]{1,0:T(8,128)S(1)}, f32[1024,512]{1,0:T(8,128)S(1)}, u32[]{:S(2)}, u32[]{:S(2)}) collective-permute-start(f32[1024,512]{1,0:T(8,128)S(1)} %bitcast_add_fusion), channel_id=1, source_target_pairs={{0,1},{1,2},{2,3},{3,4},{4,5},{5,6},{6,7},{8,9},{9,10},{10,11},{11... | collective-permute-start | bytes 6291464 | tf_op jit(solution)/shard_map/ppermute | solution.py:12
  37.0 30.0 %copy-start.8 = (f32[2,3,512]{2,0,1:T(2,128)S(1)}, f32[2,3,512]{2,0,1:T(2,128)}, u32[]{:S(2)}) copy-start(f32[2,3,512]{2,0,1:T(2,128)} %param.13) | copy-start | bytes 36868
  42.0 69.7 %collective-permute-start.2 = (f32[1024,512]{1,0:T(8,128)S(1)}, f32[1024,512]{1,0:T(8,128)S(1)}, u32[]{:S(2)}, u32[]{:S(2)}) collective-permute-start(f32[1024,512]{1,0:T(8,128)S(1)} %tanh_add_fusion.5), channel_id=1, source_target_pairs={{0,2},{1,3},{2,4},{3,5},{4,6},{5,7},{8,10},{9,11},{10,12},{11,13},... | collective-permute-start | bytes 6291464 | tf_op jit(solution)/shard_map/ppermute | solution.py:12
  111.7 5.1 %copy-start.5 = (f32[2,512,512]{2,1,0:T(8,128)S(1)}, f32[2,512,512]{2,1,0:T(8,128)}, u32[]{:S(2)}) copy-start(f32[2,512,512]{2,1,0:T(8,128)} %param.10) | copy-start | bytes 6291460
  121.6 298.4 %all-reduce.5.cloned.1.call-start = ((), (), s32[]{:S(2)}) async-start(), calls=%async_computation.1 | async-start | bytes 4194304 | tf_op jit(solution)/shard_map/psum | solution.py:57
  209.6 5.5 %copy-start.3 = (f32[2,1024,512]{2,1,0:T(8,128)S(1)}, f32[2,1024,512]{2,1,0:T(8,128)}, u32[]{:S(2)}) copy-start(f32[2,1024,512]{2,1,0:T(8,128)} %param.12) | copy-start | bytes 12582916
  215.1 3.6 copy-start
  222.6 6.7 %collective-permute-start.3 = (f32[512,512]{1,0:T(8,128)S(1)}, f32[512,512]{1,0:T(8,128)S(1)}, u32[]{:S(2)}, u32[]{:S(2)}) collective-permute-start(f32[512,512]{1,0:T(8,128)S(1)} %get-tuple-element.5), channel_id=1, source_target_pairs={{0,1},{1,2},{2,3},{3,4},{4,5},{5,6},{6,7},{8,9},{9,10},{10,11},{11... | collective-permute-start | bytes 3145736 | tf_op jit(solution)/shard_map/ppermute | solution.py:12
  234.2 15.3 %collective-permute-start.4 = (f32[1024,512]{1,0:T(8,128)S(1)}, f32[1024,512]{1,0:T(8,128)S(1)}, u32[]{:S(2)}, u32[]{:S(2)}) collective-permute-start(f32[1024,512]{1,0:T(8,128)S(1)} %tanh_add_fusion.2), channel_id=1, source_target_pairs={{0,1},{1,2},{2,3},{3,4},{4,5},{5,6},{6,7},{8,9},{9,10},{10,11},{11... | collective-permute-start | bytes 6291464 | tf_op jit(solution)/shard_map/ppermute | solution.py:12
  254.4 69.9 %collective-permute-start.5 = (f32[1024,512]{1,0:T(8,128)S(1)}, f32[1024,512]{1,0:T(8,128)S(1)}, u32[]{:S(2)}, u32[]{:S(2)}) collective-permute-start(f32[1024,512]{1,0:T(8,128)S(1)} %tanh_add_fusion.1), channel_id=1, source_target_pairs={{0,2},{1,3},{2,4},{3,5},{4,6},{5,7},{8,10},{9,11},{10,12},{11,13},... | collective-permute-start | bytes 6291464 | tf_op jit(solution)/shard_map/ppermute | solution.py:12
  324.4 5.1 %copy-start.6 = (f32[2,512,512]{2,1,0:T(8,128)S(1)}, f32[2,512,512]{2,1,0:T(8,128)}, u32[]{:S(2)}) copy-start(f32[2,512,512]{2,1,0:T(8,128)} %param.10) | copy-start | bytes 6291460
  420.0 5.8 %copy-start.4 = (f32[2,1024,512]{2,1,0:T(8,128)S(1)}, f32[2,1024,512]{2,1,0:T(8,128)}, u32[]{:S(2)}) copy-start(f32[2,1024,512]{2,1,0:T(8,128)} %param.12) | copy-start | bytes 12582916
  425.8 3.6 copy-start.1
Sparse Core Ops, SparseCore 0:
  121.7 87.8 all-reduce.2
  334.4 85.5 all-reduce.4
where the time goes:
time: 448 us; the launch traced here: 442 us
  waiting for transfers between devices  253 us (56%)
  matrix products  94.6 us (21%)
  starting transfers between devices  77.5 us (17%)
  between operations  14.2 us (3%)
    psum x2, waiting for transfers between devices, body(): summed = lax.psum(mapped, 'mic')  173 us
    dot_general x20, matrix products, matmul(): jnp.dot(left, right, precision=lax.Precision.HIGHEST, preferred_element_t...  94.6 us
    ppermute x6, waiting for transfers between devices, from_behind(): return lax.ppermute(x, axis, pairs)  79.9 us
    ppermute x6, starting transfers between devices, from_behind(): return lax.ppermute(x, axis, pairs)  77 us
  transfers between devices with their start and end apart: 8, of which 4 were waited for; matrix products, arithmetic and copies ran while one was open for 6% of the time, Pallas kernels for 0%

commit v1 on v0

v1 whole, which is shorter than its diff:
```python
import jax
import jax.numpy as jnp
from jax import lax
from jax.sharding import PartitionSpec as P

AXES = ("mic", "tm")


def matmul(left, right):
    return jnp.dot(left, right, precision=lax.Precision.HIGH, preferred_element_type=jnp.float32)


def delay(values, steps):
    padding = jnp.zeros(values.shape[:1] + (steps,) + values.shape[2:], values.dtype)
    return jnp.concatenate([padding, values[:, : values.shape[1] - steps]], axis=1)


def body(
    signal,
    conv_weight,
    conv_bias,
    transform_in,
    transform_mid,
    transform_out,
    transform_offsets_bias,
):
    _, frames, channels = signal.shape
    sections, layers = conv_weight.shape[:2]
    half = frames // 2
    mics = lax.axis_size("mic")
    chains = lax.all_to_all(
        signal[0].reshape(2, half, channels), AXES, split_axis=1, concat_axis=0, tiled=True
    )
    hidden = chains.reshape(mics, -1, chains.shape[1], channels)
    for s in range(sections):
        for l in range(layers):
            delayed = delay(hidden, 2**l)
            hidden = hidden + jnp.tanh(
                matmul(hidden, conv_weight[s, l, 0])
                + matmul(delayed, conv_weight[s, l, 1])
                + conv_bias[s, l]
            )
        mapped = jnp.tanh(matmul(hidden, transform_in[s]) + transform_offsets_bias[s, 0])
        average = jnp.sum(mapped, axis=0) / jnp.float32(mics)
        pooled = jnp.tanh(matmul(average, transform_mid[s]) + transform_offsets_bias[s, 1])
        mixing = (
            matmul(mapped, transform_out[s, :channels])
            + matmul(pooled, transform_out[s, channels:])
            + transform_offsets_bias[s, 2]
        )
        hidden = hidden + jnp.tanh(mixing)
    back = lax.all_to_all(
        hidden.reshape(chains.shape), AXES, split_axis=0, concat_axis=1, tiled=True
    )
    return back.reshape(1, frames, channels)


def solution(mesh):
    placed = (P("mic", "tm", None), P(), P(), P(), P(), P(), P())
    return jax.shard_map(
        body, mesh=mesh, in_specs=placed, out_specs=P("mic", "tm", None), check_vma=False
    )
```

time: 448 us -> 153 us (0.34)
  the two profiles are of different devices: /device:TPU:0 before, /device:TPU:17 now
where the time goes in v1:
time: 153 us; the launch traced here: 151 us
  blocking collectives  52.9 us (35%)
  waiting for transfers between devices  47.2 us (31%)
  matrix products  36.6 us (24%)
  local copies, waits for them, and re-layouts  7.54 us (5%)
  starting transfers between devices  6.25 us (4%)
    all_to_all x1, blocking collectives, body(): lax.all_to_all(hidden.reshape(chains.shape), AXES, split_axis=0, concat_a...  52.9 us
    all_to_all x1, waiting for transfers between devices, body(): lax.all_to_all(signal[0].reshape(2, half, channels), AXES, split_axis=1,...  47.2 us
    dot_general x20, matrix products, matmul(): jnp.dot(left, right, precision=lax.Precision.HIGH, preferred_element_type...  36.6 us
    all_to_all x1, starting transfers between devices, body(): lax.all_to_all(signal[0].reshape(2, half, channels), AXES, split_axis=1,...  6.25 us
    another operation x1, local copies, waits for them, and re-layouts, body(): signal[0].reshape(2, half, channels)  4.53 us
  transfers between devices with their start and end apart: 1, of which 1 were waited for; matrix products, arithmetic and copies ran while one was open for 0% of the time, Pallas kernels for 0%

profile of v1, /device:TPU:17, one launch (start us, length us, event | category | flops | bytes accessed | tf_op | source)
XLA Modules:
  0.0 150.7 jit_solution(13654682412371393505)
XLA Ops:
  0.0 4.5 %copy.14 = f32[2,512,512]{2,0,1:T(2,128)} copy(f32[2,512,512]{2,1,0:T(8,128)} %bitcast.172) | data formatting | bytes 4194304 | tf_op jit(solution)/shard_map/reshape;squeeze | solution.py:32
  4.5 6.2 %all-to-all-start = ((f32[2,512,512]{2,0,1:T(2,128)}), f32[2,512,512]{2,0,1:T(2,128)S(1)}, u32[]{:S(2)}, u32[]{:S(2)}) async-start(f32[2,512,512]{2,0,1:T(2,128)} %copy.14), calls=%async_computation | async-start | bytes 4194304 | tf_op jit(solution)/shard_map/all_to_all | solution.py:31
  10.8 47.2 %all-to-all-done = f32[2,512,512]{2,0,1:T(2,128)S(1)} async-done(((f32[2,512,512]{2,0,1:T(2,128)}), f32[2,512,512]{2,0,1:T(2,128)S(1)}, u32[]{:S(2)}, u32[]{:S(2)}) %all-to-all-start) | async-done | bytes 2097184 | tf_op jit(solution)/shard_map/all_to_all | solution.py:31
  58.7 3.5 %fusion.46 = f32[4,16,16,512]{3,2,1,0:T(8,128)S(1)} fusion(f32[2,3,2,512,512]{4,3,2,1,0:T(8,128)} %param.8, f32[4,16,16,512]{3,2,1,0:T(8,128)S(1)} %bitcast.167), kind=kOutput, calls=%fused_computation.50 | convolution fusion | flops 1610612736 | bytes 5242880 | tf_op jit(solution)/shard_map/dot_general | solution.py:10
  62.2 0.8 copy-done
  63.0 2.1 %tanh_add_fusion.7 = f32[4,16,16,512]{3,2,1,0:T(8,128)S(1)} fusion(f32[4,16,16,512]{3,2,1,0:T(8,128)S(1)} %bitcast.168, f32[4,16,16,512]{3,2,1,0:T(8,128)S(1)} %fusion.46, f32[512]{0:T(512)S(1)} %bitcast.186, f32[2,3,2,512,512]{4,3,2,1,0:T(8,128)S(1)} %copy-done), kind=kOutput, calls=%fused_computation.9 | convolution fusion | flops 1511522304 | bytes 9308160 | tf_op jit(solution)/shard_map/dot_general | solution.py:10
  65.1 1.9 %fusion.43 = f32[4,16,16,512]{3,2,1,0:T(8,128)S(1)} fusion(f32[4,16,16,512]{3,2,1,0:T(8,128)S(1)} %tanh_add_fusion.7, f32[2,3,2,512,512]{4,3,2,1,0:T(8,128)S(1)} %copy-done), kind=kOutput, calls=%fused_computation.47 | convolution fusion | flops 1610612736 | bytes 5242880 | tf_op jit(solution)/shard_map/dot_general | solution.py:10
  67.0 2.1 %tanh_add_fusion.6 = f32[4,16,16,512]{3,2,1,0:T(8,128)S(1)} fusion(f32[4,16,16,512]{3,2,1,0:T(8,128)S(1)} %tanh_add_fusion.7, f32[4,16,16,512]{3,2,1,0:T(8,128)S(1)} %fusion.43, f32[512]{0:T(512)S(1)} %bitcast.185, f32[2,3,2,512,512]{4,3,2,1,0:T(8,128)S(1)} %copy-done), kind=kOutput, calls=%fused_computation.8 | convolution fusion | flops 1410859008 | bytes 9177088 | tf_op jit(solution)/shard_map/dot_general | solution.py:10
  69.1 1.9 %fusion.40 = f32[4,16,16,512]{3,2,1,0:T(8,128)S(1)} fusion(f32[4,16,16,512]{3,2,1,0:T(8,128)S(1)} %tanh_add_fusion.6, f32[2,3,2,512,512]{4,3,2,1,0:T(8,128)S(1)} %copy-done), kind=kOutput, calls=%fused_computation.44 | convolution fusion | flops 1610612736 | bytes 5242880 | tf_op jit(solution)/shard_map/dot_general | solution.py:10
  71.0 2.1 %tanh_add_fusion.5 = f32[4,16,16,512]{3,2,1,0:T(8,128)S(1)} fusion(f32[4,16,16,512]{3,2,1,0:T(8,128)S(1)} %tanh_add_fusion.6, f32[4,16,16,512]{3,2,1,0:T(8,128)S(1)} %fusion.40, f32[512]{0:T(512)S(1)} %bitcast.178, f32[2,3,2,512,512]{4,3,2,1,0:T(8,128)S(1)} %copy-done), kind=kOutput, calls=%fused_computation.7 | convolution fusion | flops 1209532416 | bytes 8914944 | tf_op jit(solution)/shard_map/dot_general | solution.py:10
  73.1 2.1 %fusion.8 = (f32[16,16,512]{2,1,0:T(8,128)S(1)}, f32[4,16,16,512]{3,2,1,0:T(8,128)S(1)}) fusion(f32[512]{0:T(512)S(1)} %bitcast.175, f32[4,16,16,512]{3,2,1,0:T(8,128)S(1)} %tanh_add_fusion.5, f32[2,512,512]{2,1,0:T(8,128)S(1)} %copy-done.3), kind=kOutput, calls=%fused_computation.14 | convolution fusion | flops 1611530240 | bytes 5769216 | tf_op jit(solution)/shard_map/dot_general | solution.py:10
  75.2 0.7 fusion.23
  76.6 2.1 %tanh_add_fusion.4 = f32[4,16,16,512]{3,2,1,0:T(8,128)S(1)} fusion(f32[4,16,16,512]{3,2,1,0:T(8,128)S(1)} %tanh_add_fusion.5, f32[4,16,16,512]{3,2,1,0:T(8,128)S(1)} %get-tuple-element.18, f32[512]{0:T(512)S(1)} %bitcast.181, f32[16,16,512]{2,1,0:T(8,128)S(1)} %fusion.51, f32[2,1024,512]{2,1,0:T(8,128)S(1)} %copy-done.1, f32[512]{0:T(512)S(1)} %bitcast.176), kind=kOutput, calls=%fused_computation.5 | convolution fusion | flops 1612709888 | bytes 7868416 | tf_op jit(solution)/shard_map/dot_general | solution.py:10
  78.7 1.9 %fusion.34 = f32[4,16,16,512]{3,2,1,0:T(8,128)S(1)} fusion(f32[4,16,16,512]{3,2,1,0:T(8,128)S(1)} %tanh_add_fusion.4, f32[2,3,2,512,512]{4,3,2,1,0:T(8,128)S(1)} %copy-done), kind=kOutput, calls=%fused_computation.38 | convolution fusion | flops 1610612736 | bytes 5242880 | tf_op jit(solution)/shard_map/dot_general | solution.py:10
  80.6 2.1 %tanh_add_fusion.3 = f32[4,16,16,512]{3,2,1,0:T(8,128)S(1)} fusion(f32[4,16,16,512]{3,2,1,0:T(8,128)S(1)} %tanh_add_fusion.4, f32[4,16,16,512]{3,2,1,0:T(8,128)S(1)} %fusion.34, f32[512]{0:T(512)S(1)} %bitcast.184, f32[2,3,2,512,512]{4,3,2,1,0:T(8,128)S(1)} %copy-done), kind=kOutput, calls=%fused_computation.4 | convolution fusion | flops 1511522304 | bytes 9308160 | tf_op jit(solution)/shard_map/dot_general | solution.py:10
  82.7 1.9 %fusion.31 = f32[4,16,16,512]{3,2,1,0:T(8,128)S(1)} fusion(f32[4,16,16,512]{3,2,1,0:T(8,128)S(1)} %tanh_add_fusion.3, f32[2,3,2,512,512]{4,3,2,1,0:T(8,128)S(1)} %copy-done), kind=kOutput, calls=%fused_computation.35 | convolution fusion | flops 1610612736 | bytes 5242880 | tf_op jit(solution)/shard_map/dot_general | solution.py:10
  84.6 2.1 %tanh_add_fusion.2 = f32[4,16,16,512]{3,2,1,0:T(8,128)S(1)} fusion(f32[4,16,16,512]{3,2,1,0:T(8,128)S(1)} %tanh_add_fusion.3, f32[4,16,16,512]{3,2,1,0:T(8,128)S(1)} %fusion.31, f32[512]{0:T(512)S(1)} %bitcast.183, f32[2,3,2,512,512]{4,3,2,1,0:T(8,128)S(1)} %copy-done), kind=kOutput, calls=%fused_computation.3 | convolution fusion | flops 1410859008 | bytes 9177088 | tf_op jit(solution)/shard_map/dot_general | solution.py:10
  86.7 2.1 %fusion.28 = f32[4,16,16,512]{3,2,1,0:T(8,128)S(1)} fusion(f32[4,16,16,512]{3,2,1,0:T(8,128)S(1)} %tanh_add_fusion.2, f32[2,3,2,512,512]{4,3,2,1,0:T(8,128)S(1)} %copy-done), kind=kOutput, calls=%fused_computation.32 | convolution fusion | flops 1610612736 | bytes 5242880 | tf_op jit(solution)/shard_map/dot_general | solution.py:10
  88.8 2.1 %tanh_add_fusion.1 = f32[4,16,16,512]{3,2,1,0:T(8,128)S(1)} fusion(f32[4,16,16,512]{3,2,1,0:T(8,128)S(1)} %tanh_add_fusion.2, f32[4,16,16,512]{3,2,1,0:T(8,128)S(1)} %fusion.28, f32[512]{0:T(512)S(1)} %bitcast.177, f32[2,3,2,512,512]{4,3,2,1,0:T(8,128)S(1)} %copy-done), kind=kOutput, calls=%fused_computation.2 | convolution fusion | flops 1209532416 | bytes 8914944 | tf_op jit(solution)/shard_map/dot_general | solution.py:10
  90.9 1.9 %fusion.10 = (f32[16,16,512]{2,1,0:T(8,128)S(1)}, f32[4,16,16,512]{3,2,1,0:T(8,128)S(1)}) fusion(f32[512]{0:T(512)S(1)} %bitcast.173, f32[4,16,16,512]{3,2,1,0:T(8,128)S(1)} %tanh_add_fusion.1, f32[2,512,512]{2,1,0:T(8,128)S(1)} %copy-done.3), kind=kOutput, calls=%fused_computation.16 | convolution fusion | flops 1611530240 | bytes 5769216 | tf_op jit(solution)/shard_map/dot_general | solution.py:10
  92.8 0.7 fusion.22
  94.2 2.1 %tanh_add_fusion = f32[4,16,16,512]{3,2,1,0:T(8,128)S(1)} fusion(f32[4,16,16,512]{3,2,1,0:T(8,128)S(1)} %tanh_add_fusion.1, f32[4,16,16,512]{3,2,1,0:T(8,128)S(1)} %get-tuple-element.20, f32[512]{0:T(512)S(1)} %bitcast.179, f32[16,16,512]{2,1,0:T(8,128)S(1)} %fusion.48, f32[2,1024,512]{2,1,0:T(8,128)S(1)} %copy-done.1, f32[512]{0:T(512)S(1)} %bitcast.174), kind=kOutput, calls=%fused_computation | convolution fusion | flops 1612709888 | bytes 7868416 | tf_op jit(solution)/shard_map/dot_general | solution.py:10
  96.3 52.9 %all_to_all.30 = f32[64,16,512]{2,1,0:T(8,128)S(1)} all-to-all(f32[64,16,512]{2,1,0:T(8,128)S(1)} %bitcast.169), channel_id=1, replica_groups=mesh['mic'=4,'tm'=8] {'mic','tm'}, dimensions={0} | all-to-all | bytes 4194304 | tf_op jit(solution)/shard_map/all_to_all | solution.py:52
  149.2 1.6 %copy.17 = f32[32,2,16,512]{3,2,0,1:T(8,128)} copy(f32[32,2,16,512]{3,2,1,0:T(8,128)S(1)} %bitcast.171) | data formatting | bytes 4194304 | tf_op jit(solution)/shard_map/all_to_all | solution.py:52
  (17 shorter events, 1.9 us)
Async XLA Ops:
  4.5 6.3 %copy-start.4 = (f32[2,3,512]{2,0,1:T(2,128)S(1)}, f32[2,3,512]{2,0,1:T(2,128)}, u32[]{:S(2)}) copy-start(f32[2,3,512]{2,0,1:T(2,128)} %param.9) | copy-start | bytes 36868
  4.5 6.3 %copy-start.5 = (f32[2,3,512]{2,0,1:T(2,128)S(1)}, f32[2,3,512]{2,0,1:T(2,128)}, u32[]{:S(2)}) copy-start(f32[2,3,512]{2,0,1:T(2,128)} %param.13) | copy-start | bytes 36868
  4.5 53.5 %all-to-all-start = ((f32[2,512,512]{2,0,1:T(2,128)}), f32[2,512,512]{2,0,1:T(2,128)S(1)}, u32[]{:S(2)}, u32[]{:S(2)}) async-start(f32[2,512,512]{2,0,1:T(2,128)} %copy.14), calls=%async_computation | async-start | bytes 4194304 | tf_op jit(solution)/shard_map/all_to_all | solution.py:31
  58.1 4.9 %copy-start = (f32[2,3,2,512,512]{4,3,2,1,0:T(8,128)S(1)}, f32[2,3,2,512,512]{4,3,2,1,0:T(8,128)}, u32[]{:S(2)}) copy-start(f32[2,3,2,512,512]{4,3,2,1,0:T(8,128)} %param.8) | copy-start | bytes 37748740
  70.9 2.1 %copy-start.3 = (f32[2,512,512]{2,1,0:T(8,128)S(1)}, f32[2,512,512]{2,1,0:T(8,128)}, u32[]{:S(2)}) copy-start(f32[2,512,512]{2,1,0:T(8,128)} %param.10) | copy-start | bytes 6291460
  70.9 4.3 %copy-start.2 = (f32[2,512,512]{2,1,0:T(8,128)S(1)}, f32[2,512,512]{2,1,0:T(8,128)}, u32[]{:S(2)}) copy-start(f32[2,512,512]{2,1,0:T(8,128)} %param.11) | copy-start | bytes 6291460
  73.1 2.8 %copy-start.1 = (f32[2,1024,512]{2,1,0:T(8,128)S(1)}, f32[2,1024,512]{2,1,0:T(8,128)}, u32[]{:S(2)}) copy-start(f32[2,1024,512]{2,1,0:T(8,128)} %param.12) | copy-start | bytes 12582916

commit v2 on v1

--- a/solution.py
+++ b/solution.py
@@ -1,9 +1,15 @@
+import functools
+
 import jax
 import jax.numpy as jnp
 from jax import lax
+from jax.experimental import pallas as pl
+from jax.experimental.pallas import tpu as pltpu
 from jax.sharding import PartitionSpec as P
 
 AXES = ("mic", "tm")
+ROWS = 8
+MESH = pl.DeviceIdType.MESH
 
 
 def matmul(left, right):
@@ -55,8 +61,304 @@
     return back.reshape(1, frames, channels)
 
 
+def split(values):
+    high = values.astype(jnp.bfloat16)
+    return high, (values - high.astype(jnp.float32)).astype(jnp.bfloat16)
+
+
+def dot(left, right):
+    return jnp.dot(left, right, preferred_element_type=jnp.float32)
+
+
+def kernel(
+    chunks,
+    sections,
+    layers,
+    x_ref,
+    conv_hbm,
+    in_hbm,
+    mid_hbm,
+    out_hbm,
+    conv_bias,
+    offsets,
+    y_ref,
+    hidden,
+    act_a,
+    act_b,
+    act_u,
+    act_v,
+    mixed,
+    conv_f32,
+    one_f32,
+    conv_w,
+    in_w,
+    mid_w,
+    out_w,
+    send_sem,
+    recv_sem,
+    back_send_sem,
+    back_recv_sem,
+    weight_sem,
+):
+    mics, tms = lax.axis_size("mic"), lax.axis_size("tm")
+    devices = mics * tms
+    my_mic, my_tm = lax.axis_index("mic"), lax.axis_index("tm")
+    me = my_mic * tms + my_tm
+    share = chunks * ROWS
+    channels = x_ref.shape[2]
+    blocks = 2 * tms
+    rows = blocks * mics * ROWS
+    pad = act_a.shape[0] - rows
+
+    order = sorted(range(mics), key=lambda j: -min(j, mics - j))
+
+    def others(act):
+        for jm in order:
+            def one(jt, carry, jm=jm):
+                act(lax.rem(my_mic + jm, mics), lax.rem(my_tm + jt, tms))
+                return carry
+
+            lax.fori_loop(1 if jm == 0 else 0, tms, one, 0)
+
+    barrier = pltpu.get_barrier_semaphore()
+    others(
+        lambda m, t: pl.semaphore_signal(barrier, inc=1, device_id=(m, t), device_id_type=MESH)
+    )
+    pl.semaphore_wait(barrier, devices - 1)
+
+    def residues(owner, k):
+        return pl.ds(pl.multiple_of(owner * share + k * ROWS, ROWS), ROWS)
+
+    for k in range(chunks):
+        def send(m, t, k=k):
+            pltpu.make_async_remote_copy(
+                src_ref=x_ref.at[:, residues(m * tms + t, k)],
+                dst_ref=hidden.at[k, pl.ds(2 * my_tm, 2), my_mic],
+                send_sem=send_sem,
+                recv_sem=recv_sem.at[k],
+                device_id=(m, t),
+                device_id_type=MESH,
+            ).start()
+
+        others(send)
+        pltpu.make_async_copy(
+            x_ref.at[:, residues(me, k)],
+            hidden.at[k, pl.ds(2 * my_tm, 2), my_mic],
+            recv_sem.at[k],
+        ).start()
+
+    conv_copy = pltpu.make_async_copy(conv_hbm, conv_f32, weight_sem.at[0])
+    conv_copy.start()
+    loads = []
+    first = 0
+    for n, source in enumerate((in_hbm, mid_hbm, out_hbm)):
+        count = source.shape[0]
+        copy = pltpu.make_async_copy(source, one_f32.at[pl.ds(first, count)], weight_sem.at[1 + n])
+        copy.start()
+        loads.append((copy, first, count))
+        first += count
+    act_a[pl.ds(0, pad), :] = jnp.zeros((pad, 2 * channels), jnp.bfloat16)
+    act_b[pl.ds(0, pad), :] = jnp.zeros((pad, 2 * channels), jnp.bfloat16)
+
+    step = 64
+
+    def split_into(source, index, target, place, high_row, low_row):
+        def part(i, carry):
+            at = pl.multiple_of(i * step, step)
+            high, low = split(source[index, pl.ds(at, step), :])
+            target[place, pl.ds(pl.multiple_of(high_row + at, step), step), :] = high
+            target[place, pl.ds(pl.multiple_of(low_row + at, step), step), :] = low
+            return carry
+
+        lax.fori_loop(0, channels // step, part, 0)
+
+    conv_copy.wait()
+
+    def conv_split(n, carry):
+        for tap in range(2):
+            split_into(conv_f32, 2 * n + tap, conv_w, n, tap * channels, (2 + tap) * channels)
+        return carry
+
+    lax.fori_loop(0, sections * layers, conv_split, 0)
+    for (copy, first, count), target in zip(loads, (in_w, mid_w, out_w)):
+        copy.wait()
+
+        def other_split(n, carry, first=first, target=target):
+            split_into(one_f32, first + n, target, n, 0, channels)
+            return carry
+
+        lax.fori_loop(0, count, other_split, 0)
+
+    width = min(channels, 256)
+    body = pl.ds(pad, rows)
+
+    def product(act, part, weight, n, cols):
+        high = act[part, pl.ds(0, channels)]
+        low = act[part, pl.ds(channels, channels)]
+        return dot(jnp.concatenate([high, high], axis=1), weight[n, :, cols]) + dot(
+            low, weight[n, pl.ds(0, channels), cols]
+        )
+
+    def store(act, part, values, at):
+        high, low = split(values)
+        act[part, pl.ds(at, width)] = high
+        act[part, pl.ds(channels + at, width)] = low
+
+    def chunk(k, carry):
+        pltpu.make_async_copy(hidden.at[k], hidden.at[k], recv_sem.at[k]).wait()
+        for at in range(0, channels, width):
+            now = hidden[k, :, :, :, pl.ds(at, width)].reshape(rows, width)
+            store(act_a, body, now, at)
+
+        def section(s, carry):
+            here, there = act_a, act_b
+            for l in range(layers):
+                late = pl.ds(pad - 2**l * mics * ROWS, rows)
+                n = s * layers + l
+                for at in range(0, channels, width):
+                    cols = pl.ds(at, width)
+                    high = here[body, pl.ds(0, channels)]
+                    late_high = here[late, pl.ds(0, channels)]
+                    low = here[body, pl.ds(channels, channels)]
+                    late_low = here[late, pl.ds(channels, channels)]
+                    total = dot(
+                        jnp.concatenate([high, late_high, high, late_high], axis=1),
+                        conv_w[n, :, cols],
+                    ) + dot(
+                        jnp.concatenate([low, late_low], axis=1),
+                        conv_w[n, pl.ds(0, 2 * channels), cols],
+                    )
+                    new = hidden[k, :, :, :, cols].reshape(rows, width) + jnp.tanh(
+                        total + conv_bias[n, :, cols]
+                    )
+                    hidden[k, :, :, :, cols] = new.reshape(blocks, mics, ROWS, width)
+                    store(there, body, new, at)
+                here, there = there, here
+            every = pl.ds(0, blocks * ROWS)
+            for at in range(0, channels, width):
+                cols = pl.ds(at, width)
+                mapped = jnp.tanh(product(here, body, in_w, s, cols) + offsets[3 * s, :, cols])
+                store(act_u, pl.ds(0, rows), mapped, at)
+                average = jnp.sum(
+                    mapped.reshape(blocks, mics, ROWS, width), axis=1
+                ) / jnp.float32(mics)
+                store(act_v, every, average.reshape(blocks * ROWS, width), at)
+            for at in range(0, channels, width):
+                cols = pl.ds(at, width)
+                pooled = jnp.tanh(
+                    product(act_v, every, mid_w, s, cols) + offsets[3 * s + 1, :, cols]
+                )
+                store(mixed, every, pooled, at)
+            for at in range(0, channels, width):
+                cols = pl.ds(at, width)
+                shared = product(mixed, every, out_w, 2 * s + 1, cols) + offsets[3 * s + 2, :, cols]
+                mixing = product(act_u, pl.ds(0, rows), out_w, 2 * s, cols).reshape(
+                    blocks, mics, ROWS, width
+                ) + shared.reshape(blocks, 1, ROWS, width)
+                new = hidden[k, :, :, :, cols] + jnp.tanh(mixing)
+                hidden[k, :, :, :, cols] = new
+                store(act_a, body, new.reshape(rows, width), at)
+            return carry
+
+        lax.fori_loop(0, sections, section, 0)
+
+        def send_back(m, t):
+            pltpu.make_async_remote_copy(
+                src_ref=hidden.at[k, pl.ds(2 * t, 2), m],
+                dst_ref=y_ref.at[:, residues(me, k)],
+                send_sem=back_send_sem,
+                recv_sem=back_recv_sem,
+                device_id=(m, t),
+                device_id_type=MESH,
+            ).start()
+
+        others(send_back)
+        pltpu.make_async_copy(
+            hidden.at[k, pl.ds(2 * my_tm, 2), my_mic],
+            y_ref.at[:, residues(me, k)],
+            back_recv_sem,
+        ).start()
+        return carry
+
+    lax.fori_loop(0, chunks, chunk, 0)
+
+    sent = x_ref.at[:, pl.ds(0, (devices - 1) * share)]
+    pltpu.make_async_copy(sent, sent, send_sem).wait()
+    pltpu.make_async_copy(sent, sent, back_send_sem).wait()
+    pltpu.make_async_copy(y_ref, y_ref, back_recv_sem).wait()
+
+
+def fused(
+    mics,
+    tms,
+    signal,
+    conv_weight,
+    conv_bias,
+    transform_in,
+    transform_mid,
+    transform_out,
+    transform_offsets_bias,
+):
+    _, frames, channels = signal.shape
+    sections, layers = conv_weight.shape[:2]
+    half = frames // 2
+    chunks = half // (mics * tms) // ROWS
+    blocks = 2 * tms
+    rows = blocks * mics * ROWS
+    pad = 2 ** (layers - 1) * mics * ROWS
+    bf16, f32 = jnp.bfloat16, jnp.float32
+    anywhere = pl.BlockSpec(memory_space=pl.ANY)
+    vmem = pl.BlockSpec(memory_space=pltpu.VMEM)
+    out = pl.pallas_call(
+        functools.partial(kernel, chunks, sections, layers),
+        out_shape=jax.ShapeDtypeStruct((2, half, channels), f32),
+        in_specs=[anywhere] * 5 + [vmem] * 2,
+        out_specs=anywhere,
+        scratch_shapes=[
+            pltpu.VMEM((chunks, blocks, mics, ROWS, channels), f32),
+            pltpu.VMEM((pad + rows, 2 * channels), bf16),
+            pltpu.VMEM((pad + rows, 2 * channels), bf16),
+            pltpu.VMEM((rows, 2 * channels), bf16),
+            pltpu.VMEM((blocks * ROWS, 2 * channels), bf16),
+            pltpu.VMEM((blocks * ROWS, 2 * channels), bf16),
+            pltpu.VMEM((sections * layers * 2, channels, channels), f32),
+            pltpu.VMEM((sections * 4, channels, channels), f32),
+            pltpu.VMEM((sections * layers, 4 * channels, channels), bf16),
+            pltpu.VMEM((sections, 2 * channels, channels), bf16),
+            pltpu.VMEM((sections, 2 * channels, channels), bf16),
+            pltpu.VMEM((sections * 2, 2 * channels, channels), bf16),
+            pltpu.SemaphoreType.DMA,
+            pltpu.SemaphoreType.DMA((chunks,)),
+            pltpu.SemaphoreType.DMA,
+            pltpu.SemaphoreType.DMA,
+            pltpu.SemaphoreType.DMA((4,)),
+        ],
+        compiler_params=pltpu.CompilerParams(
+            collective_id=0, has_side_effects=True, vmem_limit_bytes=60 * 1024 * 1024
+        ),
+        name="sections",
+    )(
+        signal.reshape(2, half, channels),
+        conv_weight.reshape(-1, channels, channels),
+        transform_in,
+        transform_mid,
+        transform_out.reshape(-1, channels, channels),
+        conv_bias.reshape(-1, 1, channels),
+        transform_offsets_bias.reshape(-1, 1, channels),
+    )
+    return out.reshape(1, frames, channels)
+
+
 def solution(mesh):
+    mics, tms = mesh.shape["mic"], mesh.shape["tm"]
+
+    def run(signal, *parameters):
+        half = signal.shape[1] // 2
+        if half % (mics * tms * ROWS) == 0 and mics % 2 == 0:
+            return fused(mics, tms, signal, *parameters)
+        return body(signal, *parameters)
+
     placed = (P("mic", "tm", None), P(), P(), P(), P(), P(), P())
     return jax.shard_map(
-        body, mesh=mesh, in_specs=placed, out_specs=P("mic", "tm", None), check_vma=False
-    )
+        run, mesh=mesh, in_specs=placed, out_specs=P("mic", "tm", None), check_vma=False
+    )

time: 153 us -> 105 us (0.69); the launches traced: 151 us -> 105 us
  Pallas kernels: 0 us -> 99.1 us
  blocking collectives: 52.9 us -> 0 us
  waiting for transfers between devices: 47.2 us -> 0 us
  matrix products: 36.6 us -> 0 us
  starting transfers between devices: 6.25 us -> 0 us
  local copies, waits for them, and re-layouts: 7.54 us -> 5.75 us
    pallas_call x0 -> x1, Pallas kernels: none -> 99.1 us  [fused(): pl.pallas_call(functools.partial(kernel, chunks, sections, layers), out_s...]
    all_to_all x1 -> x0, blocking collectives: 52.9 us -> none  [body(): lax.all_to_all(hidden.reshape(chains.shape), AXES, split_axis=0, concat_a...]
    all_to_all x1 -> x0, waiting for transfers between devices: 47.2 us -> none  [body(): lax.all_to_all(signal[0].reshape(2, half, channels), AXES, split_axis=1,...]
    dot_general x20 -> x0, matrix products: 36.6 us -> none  [matmul(): jnp.dot(left, right, precision=lax.Precision.HIGH, preferred_element_type...]
    all_to_all x1 -> x0, starting transfers between devices: 6.25 us -> none  [body(): lax.all_to_all(signal[0].reshape(2, half, channels), AXES, split_axis=1,...]
    another operation x1 -> x0, local copies, waits for them, and re-layouts: 4.53 us -> none  [body(): signal[0].reshape(2, half, channels)]
    unnamed x12 -> x3, local copies, waits for them, and re-layouts: 0.84 us -> 4.5 us
    all_to_all x3 -> x0, local copies, waits for them, and re-layouts: 2.15 us -> none  [the longest x1 1.57 us: body(): lax.all_to_all(hidden.reshape(chains.shape), AXES, split_axis=0, concat_a...]
  transfers between devices with their start and end apart: 1 -> 0, of which waited for: 1 -> 0; matrix products, arithmetic and copies ran while one was open for 0% -> 0% of each run, Pallas kernels for 0% -> 0%
where the time goes in v2:
time: 105 us
  Pallas kernels  99.1 us (94%)
  local copies, waits for them, and re-layouts  5.75 us (5%)
    pallas_call x1, Pallas kernels, fused(): pl.pallas_call(functools.partial(kernel, chunks, sections, layers), out_s...  99.1 us
    unnamed x3, local copies, waits for them, and re-layouts  4.5 us

profile of v2, /device:TPU:17, one launch (start us, length us, event | category | flops | bytes accessed | tf_op | source)
XLA Modules:
  0.0 104.8 jit_solution(2050629782206955763)
XLA Ops:
  0.0 0.7 copy.10
  0.7 0.6 reshape.24.conv_bias
  1.3 0.7 copy.11
  2.1 0.6 reshape.25.offsets
  2.7 99.1 %sections.1 = f32[2,512,512]{2,1,0:T(8,128)} custom-call(f32[2,512,512]{2,1,0:T(8,128)} %bitcast.7, f32[12,512,512]{2,1,0:T(8,128)} %bitcast.4, f32[2,512,512]{2,1,0:T(8,128)} %in_hbm.1, f32[2,512,512]{2,1,0:T(8,128)} %mid_hbm.1, f32[4,512,512]{2,1,0:T(8,128)} %bitcast.6, f32[6,1,512]{2,1,0:T(1,128)} %reshape.24.conv_bias, f32[6,1,512]{2,1,0:T(1,128)} %reshape.25.offsets), custom_call_target="tpu_custom_call" | custom-call | tf_op jit(solution)/shard_map/sections/pallas_call | solution.py:312
  101.8 3.1 %copy.15 = f32[1,1024,512]{2,1,0:T(8,128)} copy(f32[1,1024,512]{2,1,0:T(8,128)} %bitcast.5) | data formatting | bytes 4194304

commit v3 on v2

--- a/solution.py
+++ b/solution.py
@@ -79,8 +79,8 @@
     in_hbm,
     mid_hbm,
     out_hbm,
-    conv_bias,
-    offsets,
+    conv_bias_hbm,
+    offsets_hbm,
     y_ref,
     hidden,
     act_a,
@@ -94,6 +94,8 @@
     in_w,
     mid_w,
     out_w,
+    conv_bias,
+    offsets,
     send_sem,
     recv_sem,
     back_send_sem,
@@ -120,6 +122,12 @@
 
             lax.fori_loop(1 if jm == 0 else 0, tms, one, 0)
 
+    bias_copies = [
+        pltpu.make_async_copy(conv_bias_hbm, conv_bias, weight_sem.at[4]),
+        pltpu.make_async_copy(offsets_hbm, offsets, weight_sem.at[5]),
+    ]
+    for copy in bias_copies:
+        copy.start()
     barrier = pltpu.get_barrier_semaphore()
     others(
         lambda m, t: pl.semaphore_signal(barrier, inc=1, device_id=(m, t), device_id_type=MESH)
@@ -172,6 +180,8 @@
 
         lax.fori_loop(0, channels // step, part, 0)
 
+    for copy in bias_copies:
+        copy.wait()
     conv_copy.wait()
 
     def conv_split(n, carry):
@@ -189,7 +199,7 @@
 
         lax.fori_loop(0, count, other_split, 0)
 
-    width = min(channels, 256)
+    width = channels
     body = pl.ds(pad, rows)
 
     def product(act, part, weight, n, cols):
@@ -229,7 +239,7 @@
                         conv_w[n, pl.ds(0, 2 * channels), cols],
                     )
                     new = hidden[k, :, :, :, cols].reshape(rows, width) + jnp.tanh(
-                        total + conv_bias[n, :, cols]
+                        total + conv_bias[l, pl.ds(s, 1), cols]
                     )
                     hidden[k, :, :, :, cols] = new.reshape(blocks, mics, ROWS, width)
                     store(there, body, new, at)
@@ -237,7 +247,7 @@
             every = pl.ds(0, blocks * ROWS)
             for at in range(0, channels, width):
                 cols = pl.ds(at, width)
-                mapped = jnp.tanh(product(here, body, in_w, s, cols) + offsets[3 * s, :, cols])
+                mapped = jnp.tanh(product(here, body, in_w, s, cols) + offsets[0, pl.ds(s, 1), cols])
                 store(act_u, pl.ds(0, rows), mapped, at)
                 average = jnp.sum(
                     mapped.reshape(blocks, mics, ROWS, width), axis=1
@@ -246,12 +256,12 @@
             for at in range(0, channels, width):
                 cols = pl.ds(at, width)
                 pooled = jnp.tanh(
-                    product(act_v, every, mid_w, s, cols) + offsets[3 * s + 1, :, cols]
+                    product(act_v, every, mid_w, s, cols) + offsets[1, pl.ds(s, 1), cols]
                 )
                 store(mixed, every, pooled, at)
             for at in range(0, channels, width):
                 cols = pl.ds(at, width)
-                shared = product(mixed, every, out_w, 2 * s + 1, cols) + offsets[3 * s + 2, :, cols]
+                shared = product(mixed, every, out_w, 2 * s + 1, cols) + offsets[2, pl.ds(s, 1), cols]
                 mixing = product(act_u, pl.ds(0, rows), out_w, 2 * s, cols).reshape(
                     blocks, mics, ROWS, width
                 ) + shared.reshape(blocks, 1, ROWS, width)
@@ -308,12 +318,11 @@
     pad = 2 ** (layers - 1) * mics * ROWS
     bf16, f32 = jnp.bfloat16, jnp.float32
     anywhere = pl.BlockSpec(memory_space=pl.ANY)
-    vmem = pl.BlockSpec(memory_space=pltpu.VMEM)
     out = pl.pallas_call(
         functools.partial(kernel, chunks, sections, layers),
-        out_shape=jax.ShapeDtypeStruct((2, half, channels), f32),
-        in_specs=[anywhere] * 5 + [vmem] * 2,
-        out_specs=anywhere,
+        out_shape=pltpu.VMEM((2, half, channels), f32),
+        in_specs=[anywhere] * 7,
+        out_specs=pl.BlockSpec(memory_space=pltpu.VMEM),
         scratch_shapes=[
             pltpu.VMEM((chunks, blocks, mics, ROWS, channels), f32),
             pltpu.VMEM((pad + rows, 2 * channels), bf16),
@@ -327,11 +336,13 @@
             pltpu.VMEM((sections, 2 * channels, channels), bf16),
             pltpu.VMEM((sections, 2 * channels, channels), bf16),
             pltpu.VMEM((sections * 2, 2 * channels, channels), bf16),
+            pltpu.VMEM((layers, sections, channels), f32),
+            pltpu.VMEM((3, sections, channels), f32),
             pltpu.SemaphoreType.DMA,
             pltpu.SemaphoreType.DMA((chunks,)),
             pltpu.SemaphoreType.DMA,
             pltpu.SemaphoreType.DMA,
-            pltpu.SemaphoreType.DMA((4,)),
+            pltpu.SemaphoreType.DMA((6,)),
         ],
         compiler_params=pltpu.CompilerParams(
             collective_id=0, has_side_effects=True, vmem_limit_bytes=60 * 1024 * 1024
@@ -343,8 +354,8 @@
         transform_in,
         transform_mid,
         transform_out.reshape(-1, channels, channels),
-        conv_bias.reshape(-1, 1, channels),
-        transform_offsets_bias.reshape(-1, 1, channels),
+        conv_bias.swapaxes(0, 1),
+        transform_offsets_bias.swapaxes(0, 1),
     )
     return out.reshape(1, frames, channels)
 

time: 105 us -> 99.7 us (0.950)
  local copies, waits for them, and re-layouts: 5.75 us -> 1.32 us
    unnamed x3 -> x1, local copies, waits for them, and re-layouts: 4.5 us -> 1.32 us
    reshape x2 -> x0, local copies, waits for them, and re-layouts: 1.25 us -> none  [the longest x1 0.63 us: fused(): conv_bias.reshape(-1, 1, channels)]
where the time goes in v3:
time: 99.7 us; the launch traced here: 99.5 us
  Pallas kernels  98.2 us (98%)
  local copies, waits for them, and re-layouts  1.32 us (1%)
    pallas_call x1, Pallas kernels, fused(): pl.pallas_call(functools.partial(kernel, chunks, sections, layers), out_s...  98.2 us

profile of v3, /device:TPU:17, one launch (start us, length us, event | category | flops | bytes accessed | tf_op | source)
XLA Modules:
  0.0 99.5 jit_solution(11952170854136932083)
XLA Ops:
  0.0 98.2 %sections.1 = f32[2,512,512]{2,1,0:T(8,128)S(1)} custom-call(f32[2,512,512]{2,1,0:T(8,128)} %bitcast.9, f32[12,512,512]{2,1,0:T(8,128)} %bitcast.7, f32[2,512,512]{2,1,0:T(8,128)} %in_hbm.1, f32[2,512,512]{2,1,0:T(8,128)} %mid_hbm.1, f32[4,512,512]{2,1,0:T(8,128)} %bitcast.8, f32[3,2,512]{2,1,0:T(2,128)} %bitcast.10, f32[3,2,512]{2,1,0:T(2,128)} %bitcast.11), custom_call_target="tpu_custom_call" | custom-call | tf_op jit(solution)/shard_map/sections/pallas_call | solution.py:321
  98.2 1.3 %copy.9 = f32[1,1024,512]{2,1,0:T(8,128)} copy(f32[1,1024,512]{2,1,0:T(8,128)S(1)} %bitcast.6) | data formatting | bytes 4194304

commit v4 on v3

v4 whole, which is shorter than its diff:
```python
import functools

import jax
import jax.numpy as jnp
from jax import lax
from jax.experimental import pallas as pl
from jax.experimental.pallas import tpu as pltpu
from jax.sharding import PartitionSpec as P

AXES = ("mic", "tm")
ROWS = 8
MESH = pl.DeviceIdType.MESH


def matmul(left, right):
    return jnp.dot(left, right, precision=lax.Precision.HIGH, preferred_element_type=jnp.float32)


def delay(values, steps):
    padding = jnp.zeros(values.shape[:1] + (steps,) + values.shape[2:], values.dtype)
    return jnp.concatenate([padding, values[:, : values.shape[1] - steps]], axis=1)


def body(
    signal,
    conv_weight,
    conv_bias,
    transform_in,
    transform_mid,
    transform_out,
    transform_offsets_bias,
):
    _, frames, channels = signal.shape
    sections, layers = conv_weight.shape[:2]
    half = frames // 2
    mics = lax.axis_size("mic")
    chains = lax.all_to_all(
        signal[0].reshape(2, half, channels), AXES, split_axis=1, concat_axis=0, tiled=True
    )
    hidden = chains.reshape(mics, -1, chains.shape[1], channels)
    for s in range(sections):
        for l in range(layers):
            delayed = delay(hidden, 2**l)
            hidden = hidden + jnp.tanh(
                matmul(hidden, conv_weight[s, l, 0])
                + matmul(delayed, conv_weight[s, l, 1])
                + conv_bias[s, l]
            )
        mapped = jnp.tanh(matmul(hidden, transform_in[s]) + transform_offsets_bias[s, 0])
        average = jnp.sum(mapped, axis=0) / jnp.float32(mics)
        pooled = jnp.tanh(matmul(average, transform_mid[s]) + transform_offsets_bias[s, 1])
        mixing = (
            matmul(mapped, transform_out[s, :channels])
            + matmul(pooled, transform_out[s, channels:])
            + transform_offsets_bias[s, 2]
        )
        hidden = hidden + jnp.tanh(mixing)
    back = lax.all_to_all(
        hidden.reshape(chains.shape), AXES, split_axis=0, concat_axis=1, tiled=True
    )
    return back.reshape(1, frames, channels)


def split(values):
    high = values.astype(jnp.bfloat16)
    return high, (values - high.astype(jnp.float32)).astype(jnp.bfloat16)


def dot(left, right):
    return jnp.dot(left, right, preferred_element_type=jnp.float32)


def kernel(
    chunks,
    sections,
    layers,
    x_ref,
    conv_hbm,
    in_hbm,
    mid_hbm,
    out_hbm,
    conv_bias_hbm,
    offsets_hbm,
    y_ref,
    hidden,
    act_a,
    act_b,
    act_u,
    conv_f32,
    one_f32,
    conv_w,
    in_w,
    mid_w,
    out_w,
    conv_bias,
    offsets,
    send_sem,
    recv_sem,
    back_send_sem,
    back_recv_sem,
    weight_sem,
):
    mics, tms = lax.axis_size("mic"), lax.axis_size("tm")
    devices = mics * tms
    my_mic, my_tm = lax.axis_index("mic"), lax.axis_index("tm")
    me = my_mic * tms + my_tm
    share = chunks * ROWS
    channels = x_ref.shape[2]
    blocks = 2 * tms
    rows = blocks * (mics // 2) * ROWS
    pad = act_a.shape[1] - rows

    group = mics // 2
    near = my_mic // group
    far = 1 - near
    my_place = lax.rem(my_mic, group)

    def send_each(act, to_far=True, to_near=True):
        for j in range(group):
            place = lax.rem(my_place + j, group)

            def one(jt, carry, place=place):
                t = lax.rem(my_tm + jt, tms)
                if to_far:
                    act(far, place, t)
                if to_near:
                    act(near, place, t)
                return carry

            if j == 0 and to_far:
                act(far, place, my_tm)
            lax.fori_loop(1 if j == 0 else 0, tms, one, 0)

    bias_copies = [
        pltpu.make_async_copy(conv_bias_hbm, conv_bias, weight_sem.at[4]),
        pltpu.make_async_copy(offsets_hbm, offsets, weight_sem.at[5]),
    ]
    for copy in bias_copies:
        copy.start()
    barrier = pltpu.get_barrier_semaphore()
    send_each(
        lambda g, p, t: pl.semaphore_signal(
            barrier, inc=1, device_id=(g * group + p, t), device_id_type=MESH
        )
    )
    pl.semaphore_wait(barrier, devices - 1)

    def residues(owner, k):
        return pl.ds(pl.multiple_of(owner * share + k * ROWS, ROWS), ROWS)

    def send_chunk(k):
        def send(g, p, t):
            m = g * group + p
            pltpu.make_async_remote_copy(
                src_ref=x_ref.at[:, residues(m * tms + t, k)],
                dst_ref=hidden.at[k, near, pl.ds(2 * my_tm, 2), my_place],
                send_sem=send_sem,
                recv_sem=recv_sem.at[k, near],
                device_id=(m, t),
                device_id_type=MESH,
            ).start()

        send_each(send)
        pltpu.make_async_copy(
            x_ref.at[:, residues(me, k)],
            hidden.at[k, near, pl.ds(2 * my_tm, 2), my_place],
            recv_sem.at[k, near],
        ).start()

    send_chunk(0)

    conv_copy = pltpu.make_async_copy(conv_hbm, conv_f32, weight_sem.at[0])
    conv_copy.start()
    loads = []
    first = 0
    for n, source in enumerate((in_hbm, mid_hbm, out_hbm)):
        count = source.shape[0]
        copy = pltpu.make_async_copy(source, one_f32.at[pl.ds(first, count)], weight_sem.at[1 + n])
        copy.start()
        loads.append((copy, first, count))
        first += count
    for k in range(1, chunks):
        send_chunk(k)
    for g in range(2):
        act_a[g, pl.ds(0, pad), :] = jnp.zeros((pad, 2 * channels), jnp.bfloat16)
        act_b[g, pl.ds(0, pad), :] = jnp.zeros((pad, 2 * channels), jnp.bfloat16)

    step = 64

    def split_into(source, index, target, place, high_row, low_row):
        def part(i, carry):
            at = pl.multiple_of(i * step, step)
            high, low = split(source[index, pl.ds(at, step), :])
            target[place, pl.ds(pl.multiple_of(high_row + at, step), step), :] = high
            target[place, pl.ds(pl.multiple_of(low_row + at, step), step), :] = low
            return carry

        lax.fori_loop(0, channels // step, part, 0)

    for copy in bias_copies:
        copy.wait()
    conv_copy.wait()

    def conv_split(n, carry):
        for tap in range(2):
            split_into(conv_f32, 2 * n + tap, conv_w, n, tap * channels, (2 + tap) * channels)
        return carry

    lax.fori_loop(0, sections * layers, conv_split, 0)
    body = pl.ds(pad, rows)
    high_part, low_part = pl.ds(0, channels), pl.ds(channels, channels)
    shape = (blocks, group, ROWS, channels)

    def product(high, low, weight, n):
        return dot(jnp.concatenate([high, high], axis=1), weight[n]) + dot(
            low, weight[n, pl.ds(0, channels)]
        )

    def load(act, groups, part, columns):
        return jnp.concatenate([act[g, part, columns] for g in groups], axis=0)

    def store(act, g, part, values):
        high, low = split(values)
        act[g, part, high_part] = high
        act[g, part, low_part] = low

    def convolve(k, s, groups):
        for g in groups:
            store(act_a, g, body, hidden[k, g].reshape(rows, channels))
        here, there = act_a, act_b
        for l in range(layers):
            late = pl.ds(pad - 2**l * group * ROWS, rows)
            n = s * layers + l
            high = load(here, groups, body, high_part)
            late_high = load(here, groups, late, high_part)
            low = load(here, groups, body, low_part)
            late_low = load(here, groups, late, low_part)
            total = dot(
                jnp.concatenate([high, late_high, high, late_high], axis=1), conv_w[n]
            ) + dot(
                jnp.concatenate([low, late_low], axis=1),
                conv_w[n, pl.ds(0, 2 * channels)],
            )
            delta = jnp.tanh(total + conv_bias[l, pl.ds(s, 1), :])
            for i, g in enumerate(groups):
                new = hidden[k, g] + delta[i * rows : (i + 1) * rows].reshape(shape)
                hidden[k, g] = new
                if l < layers - 1:
                    store(there, g, body, new.reshape(rows, channels))
            here, there = there, here

    def connect(k, s, send):
        high, low = split(hidden[k].reshape(2 * rows, channels))
        mapped = jnp.tanh(product(high, low, in_w, s) + offsets[0, pl.ds(s, 1), :])
        for g in range(2):
            store(act_u, g, pl.ds(0, rows), mapped[g * rows : (g + 1) * rows])
        average = jnp.sum(mapped.reshape((2,) + shape), axis=(0, 2)) / jnp.float32(mics)
        high, low = split(average.reshape(blocks * ROWS, channels))
        pooled = jnp.tanh(product(high, low, mid_w, s) + offsets[1, pl.ds(s, 1), :])
        high, low = split(pooled)
        shared = product(high, low, out_w, 2 * s + 1) + offsets[2, pl.ds(s, 1), :]
        shared = shared.reshape(blocks, 1, ROWS, channels)
        for g in (far, near):
            mixing = product(
                act_u[g, :, high_part], act_u[g, :, low_part], out_w, 2 * s
            ).reshape(shape)
            hidden[k, g] = hidden[k, g] + jnp.tanh(mixing + shared)
            if send:
                send_back(k, g is far)

    def send_back(k, to_far):
        def send(g, p, t):
            pltpu.make_async_remote_copy(
                src_ref=hidden.at[k, g, pl.ds(2 * t, 2), p],
                dst_ref=y_ref.at[:, residues(me, k)],
                send_sem=back_send_sem,
                recv_sem=back_recv_sem,
                device_id=(g * group + p, t),
                device_id_type=MESH,
            ).start()

        send_each(send, to_far=to_far, to_near=not to_far)
        if not to_far:
            pltpu.make_async_copy(
                hidden.at[k, near, pl.ds(2 * my_tm, 2), my_place],
                y_ref.at[:, residues(me, k)],
                back_recv_sem,
            ).start()

    def arrived(k, g):
        pltpu.make_async_copy(hidden.at[k, g], hidden.at[k, g], recv_sem.at[k, g]).wait()

    def early(k, carry):
        arrived(k, near)
        convolve(k, 0, (near,))
        return carry

    def chunk(k, carry):
        arrived(k, far)
        convolve(k, 0, (far,))

        def section(s, carry):
            connect(k, s, False)
            convolve(k, s + 1, (0, 1))
            return carry

        lax.fori_loop(0, sections - 1, section, 0)
        connect(k, sections - 1, True)
        return carry

    early(0, 0)
    for (copy, first, count), target in zip(loads, (in_w, mid_w, out_w)):
        copy.wait()

        def other_split(n, carry, first=first, target=target):
            split_into(one_f32, first + n, target, n, 0, channels)
            return carry

        lax.fori_loop(0, count, other_split, 0)

    lax.fori_loop(1, chunks, early, 0)
    lax.fori_loop(0, chunks, chunk, 0)

    sent = x_ref.at[:, pl.ds(0, (devices - 1) * share)]
    pltpu.make_async_copy(sent, sent, send_sem).wait()
    pltpu.make_async_copy(sent, sent, back_send_sem).wait()
    pltpu.make_async_copy(y_ref, y_ref, back_recv_sem).wait()


def fused(
    mics,
    tms,
    signal,
    conv_weight,
    conv_bias,
    transform_in,
    transform_mid,
    transform_out,
    transform_offsets_bias,
):
    _, frames, channels = signal.shape
    sections, layers = conv_weight.shape[:2]
    half = frames // 2
    chunks = half // (mics * tms) // ROWS
    blocks = 2 * tms
    group = mics // 2
    rows = blocks * group * ROWS
    pad = 2 ** (layers - 1) * group * ROWS
    bf16, f32 = jnp.bfloat16, jnp.float32
    anywhere = pl.BlockSpec(memory_space=pl.ANY)
    out = pl.pallas_call(
        functools.partial(kernel, chunks, sections, layers),
        out_shape=pltpu.VMEM((2, half, channels), f32),
        in_specs=[anywhere] * 7,
        out_specs=pl.BlockSpec(memory_space=pltpu.VMEM),
        scratch_shapes=[
            pltpu.VMEM((chunks, 2, blocks, group, ROWS, channels), f32),
            pltpu.VMEM((2, pad + rows, 2 * channels), bf16),
            pltpu.VMEM((2, pad + rows, 2 * channels), bf16),
            pltpu.VMEM((2, rows, 2 * channels), bf16),
            pltpu.VMEM((sections * layers * 2, channels, channels), f32),
            pltpu.VMEM((sections * 4, channels, channels), f32),
            pltpu.VMEM((sections * layers, 4 * channels, channels), bf16),
            pltpu.VMEM((sections, 2 * channels, channels), bf16),
            pltpu.VMEM((sections, 2 * channels, channels), bf16),
            pltpu.VMEM((sections * 2, 2 * channels, channels), bf16),
            pltpu.VMEM((layers, sections, channels), f32),
            pltpu.VMEM((3, sections, channels), f32),
            pltpu.SemaphoreType.DMA,
            pltpu.SemaphoreType.DMA((chunks, 2)),
            pltpu.SemaphoreType.DMA,
            pltpu.SemaphoreType.DMA,
            pltpu.SemaphoreType.DMA((6,)),
        ],
        compiler_params=pltpu.CompilerParams(
            collective_id=0, has_side_effects=True, vmem_limit_bytes=60 * 1024 * 1024
        ),
        name="sections",
    )(
        signal.reshape(2, half, channels),
        conv_weight.reshape(-1, channels, channels),
        transform_in,
        transform_mid,
        transform_out.reshape(-1, channels, channels),
        conv_bias.swapaxes(0, 1),
        transform_offsets_bias.swapaxes(0, 1),
    )
    return out.reshape(1, frames, channels)


def solution(mesh):
    mics, tms = mesh.shape["mic"], mesh.shape["tm"]

    def run(signal, *parameters):
        half = signal.shape[1] // 2
        if half % (mics * tms * ROWS) == 0 and mics % 4 == 0:
            return fused(mics, tms, signal, *parameters)
        return body(signal, *parameters)

    placed = (P("mic", "tm", None), P(), P(), P(), P(), P(), P())
    return jax.shard_map(
        run, mesh=mesh, in_specs=placed, out_specs=P("mic", "tm", None), check_vma=False
    )
```

time: 99.7 us -> 98.1 us (0.984)
  Pallas kernels: 98.2 us -> 96.3 us
    pallas_call x1, Pallas kernels: 98.2 us -> 96.3 us  [fused(): pl.pallas_call(functools.partial(kernel, chunks, sections, layers), out_s...]
where the time goes in v4:
time: 98.1 us; the launch traced here: 97.6 us
  Pallas kernels  96.3 us (98%)
  local copies, waits for them, and re-layouts  1.32 us (1%)
    pallas_call x1, Pallas kernels, fused(): pl.pallas_call(functools.partial(kernel, chunks, sections, layers), out_s...  96.3 us

profile of v4, /device:TPU:17, one launch (start us, length us, event | category | flops | bytes accessed | tf_op | source)
XLA Modules:
  0.0 97.6 jit_solution(10403371182793366822)
XLA Ops:
  0.0 96.3 %sections.1 = f32[2,512,512]{2,1,0:T(8,128)S(1)} custom-call(f32[2,512,512]{2,1,0:T(8,128)} %bitcast.9, f32[12,512,512]{2,1,0:T(8,128)} %bitcast.7, f32[2,512,512]{2,1,0:T(8,128)} %in_hbm.1, f32[2,512,512]{2,1,0:T(8,128)} %mid_hbm.1, f32[4,512,512]{2,1,0:T(8,128)} %bitcast.8, f32[3,2,512]{2,1,0:T(2,128)} %bitcast.10, f32[3,2,512]{2,1,0:T(2,128)} %bitcast.11), custom_call_target="tpu_custom_call" | custom-call | tf_op jit(solution)/shard_map/sections/pallas_call | solution.py:351
  96.3 1.3 %copy.9 = f32[1,1024,512]{2,1,0:T(8,128)} copy(f32[1,1024,512]{2,1,0:T(8,128)S(1)} %bitcast.6) | data formatting | bytes 4194304

commit v5 on v4

--- a/solution.py
+++ b/solution.py
@@ -115,19 +115,17 @@
     far = 1 - near
     my_place = lax.rem(my_mic, group)
 
-    def send_each(act, to_far=True, to_near=True):
+    def send_each(act):
         for j in range(group):
             place = lax.rem(my_place + j, group)
 
             def one(jt, carry, place=place):
                 t = lax.rem(my_tm + jt, tms)
-                if to_far:
-                    act(far, place, t)
-                if to_near:
-                    act(near, place, t)
+                act(far, place, t)
+                act(near, place, t)
                 return carry
 
-            if j == 0 and to_far:
+            if j == 0:
                 act(far, place, my_tm)
             lax.fori_loop(1 if j == 0 else 0, tms, one, 0)
 
@@ -249,7 +247,7 @@
                     store(there, g, body, new.reshape(rows, channels))
             here, there = there, here
 
-    def connect(k, s, send):
+    def connect(k, s):
         high, low = split(hidden[k].reshape(2 * rows, channels))
         mapped = jnp.tanh(product(high, low, in_w, s) + offsets[0, pl.ds(s, 1), :])
         for g in range(2):
@@ -260,15 +258,12 @@
         high, low = split(pooled)
         shared = product(high, low, out_w, 2 * s + 1) + offsets[2, pl.ds(s, 1), :]
         shared = shared.reshape(blocks, 1, ROWS, channels)
-        for g in (far, near):
-            mixing = product(
-                act_u[g, :, high_part], act_u[g, :, low_part], out_w, 2 * s
-            ).reshape(shape)
-            hidden[k, g] = hidden[k, g] + jnp.tanh(mixing + shared)
-            if send:
-                send_back(k, g is far)
-
-    def send_back(k, to_far):
+        high = load(act_u, (0, 1), pl.ds(0, rows), high_part)
+        low = load(act_u, (0, 1), pl.ds(0, rows), low_part)
+        mixing = product(high, low, out_w, 2 * s).reshape((2,) + shape)
+        hidden[k] = hidden[k] + jnp.tanh(mixing + shared)
+
+    def send_back(k):
         def send(g, p, t):
             pltpu.make_async_remote_copy(
                 src_ref=hidden.at[k, g, pl.ds(2 * t, 2), p],
@@ -279,13 +274,12 @@
                 device_id_type=MESH,
             ).start()
 
-        send_each(send, to_far=to_far, to_near=not to_far)
-        if not to_far:
-            pltpu.make_async_copy(
-                hidden.at[k, near, pl.ds(2 * my_tm, 2), my_place],
-                y_ref.at[:, residues(me, k)],
-                back_recv_sem,
-            ).start()
+        send_each(send)
+        pltpu.make_async_copy(
+            hidden.at[k, near, pl.ds(2 * my_tm, 2), my_place],
+            y_ref.at[:, residues(me, k)],
+            back_recv_sem,
+        ).start()
 
     def arrived(k, g):
         pltpu.make_async_copy(hidden.at[k, g], hidden.at[k, g], recv_sem.at[k, g]).wait()
@@ -300,12 +294,13 @@
         convolve(k, 0, (far,))
 
         def section(s, carry):
-            connect(k, s, False)
+            connect(k, s)
             convolve(k, s + 1, (0, 1))
             return carry
 
         lax.fori_loop(0, sections - 1, section, 0)
-        connect(k, sections - 1, True)
+        connect(k, sections - 1)
+        send_back(k)
         return carry
 
     early(0, 0)

time: 98.1 us -> 97.8 us (level)
  no operation moved by 1% of the time
where the time goes in v5:
time: 97.8 us; the launch traced here: 97.6 us
  Pallas kernels  96.3 us (98%)
  local copies, waits for them, and re-layouts  1.32 us (1%)
    pallas_call x1, Pallas kernels, fused(): pl.pallas_call(functools.partial(kernel, chunks, sections, layers), out_s...  96.3 us

profile of v5, /device:TPU:17, one launch (start us, length us, event | category | flops | bytes accessed | tf_op | source)
XLA Modules:
  0.0 97.6 jit_solution(9043712455747672655)
XLA Ops:
  0.0 96.3 %sections.1 = f32[2,512,512]{2,1,0:T(8,128)S(1)} custom-call(f32[2,512,512]{2,1,0:T(8,128)} %bitcast.9, f32[12,512,512]{2,1,0:T(8,128)} %bitcast.7, f32[2,512,512]{2,1,0:T(8,128)} %in_hbm.1, f32[2,512,512]{2,1,0:T(8,128)} %mid_hbm.1, f32[4,512,512]{2,1,0:T(8,128)} %bitcast.8, f32[3,2,512]{2,1,0:T(2,128)} %bitcast.10, f32[3,2,512]{2,1,0:T(2,128)} %bitcast.11), custom_call_target="tpu_custom_call" | custom-call | tf_op jit(solution)/shard_map/sections/pallas_call | solution.py:346
  96.3 1.3 %copy.9 = f32[1,1024,512]{2,1,0:T(8,128)} copy(f32[1,1024,512]{2,1,0:T(8,128)S(1)} %bitcast.6) | data formatting | bytes 4194304

commit v6 on v5

--- a/solution.py
+++ b/solution.py
@@ -177,8 +177,6 @@
         copy.start()
         loads.append((copy, first, count))
         first += count
-    for k in range(1, chunks):
-        send_chunk(k)
     for g in range(2):
         act_a[g, pl.ds(0, pad), :] = jnp.zeros((pad, 2 * channels), jnp.bfloat16)
         act_b[g, pl.ds(0, pad), :] = jnp.zeros((pad, 2 * channels), jnp.bfloat16)
@@ -303,6 +301,8 @@
         send_back(k)
         return carry
 
+    for k in range(1, chunks):
+        send_chunk(k)
     early(0, 0)
     for (copy, first, count), target in zip(loads, (in_w, mid_w, out_w)):
         copy.wait()

time: 97.8 us -> 98 us (level)
  no operation moved by 1% of the time
where the time goes in v6:
time: 98 us; the launch traced here: 97.6 us
  Pallas kernels  96.3 us (98%)
  local copies, waits for them, and re-layouts  1.32 us (1%)
    pallas_call x1, Pallas kernels, fused(): pl.pallas_call(functools.partial(kernel, chunks, sections, layers), out_s...  96.3 us

profile of v6, /device:TPU:17, one launch (start us, length us, event | category | flops | bytes accessed | tf_op | source)
XLA Modules:
  0.0 97.6 jit_solution(667390087319903956)
XLA Ops:
  0.0 96.3 %sections.1 = f32[2,512,512]{2,1,0:T(8,128)S(1)} custom-call(f32[2,512,512]{2,1,0:T(8,128)} %bitcast.9, f32[12,512,512]{2,1,0:T(8,128)} %bitcast.7, f32[2,512,512]{2,1,0:T(8,128)} %in_hbm.1, f32[2,512,512]{2,1,0:T(8,128)} %mid_hbm.1, f32[4,512,512]{2,1,0:T(8,128)} %bitcast.8, f32[3,2,512]{2,1,0:T(2,128)} %bitcast.10, f32[3,2,512]{2,1,0:T(2,128)} %bitcast.11), custom_call_target="tpu_custom_call" | custom-call | tf_op jit(solution)/shard_map/sections/pallas_call | solution.py:346
  96.3 1.3 %copy.9 = f32[1,1024,512]{2,1,0:T(8,128)} copy(f32[1,1024,512]{2,1,0:T(8,128)S(1)} %bitcast.6) | data formatting | bytes 4194304
